TPU v7x, 32 devices: a whole 2x2x4 slice. The times are simulated.
32 devices in a mesh: seq: 8 (over y, x, core), head: 4 (over z).
Axes of the slice: x: 2, y: 2, z: 4, core: 2. Of those that a mesh axis runs over, the one named last changes fastest.
Arguments:
- hidden: bfloat16 [1024, 3072], P('seq'), may hold values from -6 to 6
- cotangent: bfloat16 [1024, 3072], P('seq'), may hold values from -6 to 6
- mod_scale: float32 [3072], replicated, may hold values from -0.5 to 0.5
- mod_shift: float32 [3072], replicated, may hold values from -3 to 3
- branch_gate: float32 [3072], replicated, may hold values from 0.3 to 1.5
- query_weight: bfloat16 [3072, 1536], P('seq', 'head'), may hold values from -0.108253175 to 0.108253175, as said below
- key_weight: bfloat16 [3072, 1536], P('seq', 'head'), may hold values from -0.108253175 to 0.108253175, as said below
- value_weight: bfloat16 [3072, 1536], P('seq', 'head'), may hold values from -0.109375 to 0.109375
- output_weight: bfloat16 [3072, 1536], P('seq', 'head'), may hold values from -0.15625 to 0.15625
- query_gain: float32 [1536], P('head'), may hold values from 0.7 to 6.3
- key_gain: float32 [1536], P('head'), may hold values from 0.7 to 6.3
Outputs:
- hidden_grad: bfloat16 [1024, 3072], P('seq')
- outproj_grad: float32 [3072, 1536], P('seq', 'head')
Inputs may be any that keep to these rules, and one draw needn't show every extreme that they name: `query_weight`: entries of the query projection, of order 3072^-0.5. `key_weight`: entries of the key projection, of order 3072^-0.5.
All inputs are finite; a program needn't handle non-finite values.
Results may differ from a plain program's by a relative error of at most 0.028.
Values may be sent and summed in bfloat16 or wider, within the bound.
A program may use at most 128 MiB of HBM per device.

v0:
```python
import math

import jax
import jax.numpy as jnp
from jax import lax
from jax.sharding import PartitionSpec as P

HEAD_DIM = 128


EPSILON = 1e-06


def layer_normed(hidden, mod_scale, mod_shift):
    values = hidden.astype(jnp.float32)
    center = values - jnp.mean(values, axis=-1, keepdims=True)
    inverse = lax.rsqrt(jnp.mean(center * center, axis=-1, keepdims=True) + EPSILON)
    unit = center * inverse
    normed = (unit * (1.0 + mod_scale) + mod_shift).astype(jnp.bfloat16)
    return (unit, inverse, normed)


def layer_back(grad, unit, inverse, mod_scale):
    scaled = grad * (1.0 + mod_scale)
    middle = jnp.mean(scaled, axis=-1, keepdims=True)
    along = jnp.mean(scaled * unit, axis=-1, keepdims=True)
    return inverse * (scaled - middle - unit * along)


def head_norm(raw, gain, factor):
    inverse = lax.rsqrt(jnp.mean(raw * raw, axis=-1, keepdims=True) + EPSILON)
    unit = raw * inverse
    return (unit, inverse, (unit * gain * factor).astype(jnp.bfloat16))


def head_back(grad, unit, inverse, gain, factor):
    scaled = grad * gain * factor
    along = jnp.mean(scaled * unit, axis=-1, keepdims=True)
    return (inverse * (scaled - unit * along)).astype(jnp.bfloat16)


def body(
    hidden,
    cotangent,
    mod_scale,
    mod_shift,
    branch_gate,
    query_weight,
    key_weight,
    value_weight,
    output_weight,
    query_gain,
    key_gain,
):
    factor = jnp.float32(1.0 / math.sqrt(HEAD_DIM))
    rows = hidden.shape[0]
    width = query_weight.shape[1]
    heads = width // HEAD_DIM
    cube = (rows, heads, HEAD_DIM)
    query_gains = query_gain.reshape(heads, HEAD_DIM)
    key_gains = key_gain.reshape(heads, HEAD_DIM)
    unit, inverse, normed = layer_normed(hidden, mod_scale, mod_shift)
    pieces = (
        lax.all_gather(query_weight, "seq", axis=0, tiled=True),
        lax.all_gather(key_weight, "seq", axis=0, tiled=True),
        lax.all_gather(value_weight, "seq", axis=0, tiled=True),
    )
    columns = normed
    query_raw, key_raw, value_raw = tuple(
        (jnp.dot(columns, piece, preferred_element_type=jnp.float32) for piece in pieces)
    )
    query_unit, query_inverse, query = head_norm(query_raw.reshape(cube), query_gains, factor)
    key_unit, key_inverse, keys = head_norm(key_raw.reshape(cube), key_gains, jnp.float32(1.0))
    values = value_raw.reshape(cube).astype(jnp.bfloat16)
    keys_flat = keys.reshape(rows, width)
    values_flat = values.reshape(rows, width)
    whole_keys, whole_values = (
        lax.all_gather(keys_flat, "seq", axis=0, tiled=True),
        lax.all_gather(values_flat, "seq", axis=0, tiled=True),
    )
    pieces = (whole_keys, whole_values)
    top = jnp.full((heads, rows, 1), -1e30, jnp.float32)
    key_piece = pieces[0].reshape(-1, heads, HEAD_DIM)
    value_piece = pieces[1].reshape(-1, heads, HEAD_DIM)
    scores = jnp.einsum("qhd,khd->hqk", query, key_piece, preferred_element_type=jnp.float32)
    new_top = jnp.maximum(top, jnp.max(scores, axis=-1, keepdims=True))
    expo = jnp.exp(scores - new_top)
    total = jnp.sum(expo, axis=-1, keepdims=True)
    mixed = jnp.einsum(
        "hqk,khd->hqd", expo.astype(jnp.bfloat16), value_piece, preferred_element_type=jnp.float32
    )
    top, total, mixed = (new_top, total, mixed)
    mix = jnp.transpose(mixed / total, (1, 0, 2)).astype(jnp.bfloat16)
    log_total = jnp.transpose((top + jnp.log(total))[:, :, 0])
    mix_flat = mix.reshape(rows, width)
    branch_cot = (cotangent.astype(jnp.float32) * branch_gate).astype(jnp.bfloat16)
    query_full, key_full, value_full, output_full = (
        lax.all_gather(query_weight, "seq", axis=0, tiled=True),
        lax.all_gather(key_weight, "seq", axis=0, tiled=True),
        lax.all_gather(value_weight, "seq", axis=0, tiled=True),
        lax.all_gather(output_weight, "seq", axis=0, tiled=True),
    )
    columns = branch_cot
    outproj_grad = lax.psum_scatter(
        jnp.dot(columns.T, mix_flat, preferred_element_type=jnp.float32).astype(jnp.bfloat16),
        "seq",
        scatter_dimension=0,
        tiled=True,
    ).astype(jnp.float32)
    mix_grad_flat = jnp.dot(branch_cot, output_full, preferred_element_type=jnp.float32).astype(
        jnp.bfloat16
    )
    mix_grad = mix_grad_flat.reshape(cube)
    delta = jnp.sum(mix_grad.astype(jnp.float32) * mix.astype(jnp.float32), axis=-1)
    query_flat = query.reshape(rows, width)
    key_piece = whole_keys
    value_piece = whole_values
    key_piece = key_piece.reshape(-1, heads, HEAD_DIM)
    value_piece = value_piece.reshape(-1, heads, HEAD_DIM)
    scores = jnp.einsum("qhd,khd->hqk", query, key_piece, preferred_element_type=jnp.float32)
    probs = jnp.exp(scores - jnp.transpose(log_total)[:, :, None])
    prob_grad = jnp.einsum(
        "qhd,khd->hqk", mix_grad, value_piece, preferred_element_type=jnp.float32
    )
    score_grad = (probs * (prob_grad - jnp.transpose(delta)[:, :, None])).astype(jnp.bfloat16)
    query_grad = jnp.einsum(
        "hqk,khd->qhd", score_grad, key_piece, preferred_element_type=jnp.float32
    )
    pieces = (
        lax.all_gather(query_flat.astype(jnp.float32), "seq", axis=0, tiled=True).astype(
            jnp.bfloat16
        ),
        lax.all_gather(mix_grad_flat.astype(jnp.float32), "seq", axis=0, tiled=True).astype(
            jnp.bfloat16
        ),
        lax.all_gather(log_total, "seq", axis=0, tiled=True),
        lax.all_gather(delta, "seq", axis=0, tiled=True),
    )
    query_piece = pieces[0]
    grad_piece = pieces[1]
    query_piece = query_piece.reshape(-1, heads, HEAD_DIM)
    grad_piece = grad_piece.reshape(-1, heads, HEAD_DIM)
    scores = jnp.einsum("qhd,khd->hqk", query_piece, keys, preferred_element_type=jnp.float32)
    probs = jnp.exp(scores - jnp.transpose(pieces[2])[:, :, None])
    prob_grad = jnp.einsum("qhd,khd->hqk", grad_piece, values, preferred_element_type=jnp.float32)
    score_grad = (probs * (prob_grad - jnp.transpose(pieces[3])[:, :, None])).astype(jnp.bfloat16)
    key_grad = jnp.einsum(
        "hqk,qhd->khd", score_grad, query_piece, preferred_element_type=jnp.float32
    )
    value_grad = jnp.einsum(
        "hqk,qhd->khd", probs.astype(jnp.bfloat16), grad_piece, preferred_element_type=jnp.float32
    )
    key_grad, value_grad = (key_grad, value_grad)
    query_raw_grad = head_back(query_grad, query_unit, query_inverse, query_gains, factor).reshape(
        rows, width
    )
    key_raw_grad = head_back(key_grad, key_unit, key_inverse, key_gains, jnp.float32(1.0)).reshape(
        rows, width
    )
    value_raw_grad = value_grad.astype(jnp.bfloat16).reshape(rows, width)
    partial_grad = jnp.dot(query_raw_grad, query_full.T, preferred_element_type=jnp.float32)
    partial_grad = partial_grad + jnp.dot(
        key_raw_grad, key_full.T, preferred_element_type=jnp.float32
    )
    partial_grad = partial_grad + jnp.dot(
        value_raw_grad, value_full.T, preferred_element_type=jnp.float32
    )
    normed_grad = lax.psum(partial_grad.astype(jnp.bfloat16), "head").astype(jnp.float32)
    hidden_grad = layer_back(normed_grad, unit, inverse, mod_scale).astype(jnp.bfloat16)
    return (hidden_grad, outproj_grad)


def solution(mesh):
    placed = (
        P("seq", None),
        P("seq", None),
        P(),
        P(),
        P(),
        P("seq", "head"),
        P("seq", "head"),
        P("seq", "head"),
        P("seq", "head"),
        P("head"),
        P("head"),
    )
    return jax.shard_map(
        body,
        mesh=mesh,
        in_specs=placed,
        out_specs=(P("seq", None), P("seq", "head")),
        check_vma=False,
    )
```

profile of v0, /device:TPU:0, one launch (start us, length us, event | category | flops | bytes accessed | tf_op | source)
XLA Modules:
  0.0 306.0 jit_solution(317590713781400013)
XLA Ops:
  10.6 31.0 %all-gather.5.cloned.1.call-done = bf16[3072,384]{1,0:T(8,128)(2,1)} async-done(((bf16[384,384]{1,0:T(8,128)(2,1)}), bf16[3072,384]{1,0:T(8,128)(2,1)}) %all-gather.5.cloned.1.call-update) | async-done | bytes 2359312 | tf_op jit(solution)/shard_map/all_gather | solution.py:64
  41.7 2.3 fusion.42
  44.1 28.5 %all-gather.7.cloned.1.call-done = bf16[3072,384]{1,0:T(8,128)(2,1)} async-done(((bf16[384,384]{1,0:T(8,128)(2,1)}), bf16[3072,384]{1,0:T(8,128)(2,1)}) %all-gather.7.cloned.1.call-update) | async-done | bytes 2359312 | tf_op jit(solution)/shard_map/all_gather | solution.py:65
  72.6 2.3 fusion.40
  75.3 11.1 %all_gather.35 = bf16[1024,384]{1,0:T(8,128)(2,1)S(1)} all-gather(bf16[128,384]{1,0:T(8,128)(2,1)S(1)} %multiply_convert_fusion.10), channel_id=1, replica_groups=mesh['seq'=8,'head'=4] {'seq'}, dimensions={0}, use_global_device_ids=true | all-gather | bytes 884736 | tf_op jit(solution)/shard_map/all_gather | solution.py:78
  86.7 17.0 %all-gather.9.cloned.1.call-done = bf16[3072,384]{1,0:T(8,128)(2,1)} async-done(((bf16[384,384]{1,0:T(8,128)(2,1)}), bf16[3072,384]{1,0:T(8,128)(2,1)}) %all-gather.9.cloned.1.call-update) | async-done | bytes 2359312 | tf_op jit(solution)/shard_map/all_gather | solution.py:101
  103.7 2.2 convolution_convert_fusion.3
  106.7 13.3 %all_gather.41 = bf16[1024,384]{1,0:T(8,128)(2,1)} all-gather(bf16[128,384]{1,0:T(8,128)(2,1)S(1)} %convolution_convert_fusion.3), channel_id=1, replica_groups=mesh['seq'=8,'head'=4] {'seq'}, dimensions={0}, use_global_device_ids=true | all-gather | bytes 884736 | tf_op jit(solution)/shard_map/all_gather | solution.py:133
  124.0 11.5 %all-gather.11.cloned.1.call-done = bf16[3072,384]{1,0:T(8,128)(2,1)} async-done(((bf16[384,384]{1,0:T(8,128)(2,1)}), bf16[3072,384]{1,0:T(8,128)(2,1)}) %all-gather.11.cloned.1.call-update) | async-done | bytes 2359312 | tf_op jit(solution)/shard_map/all_gather | solution.py:66
  135.5 2.3 convolution_convert_fusion.2
  138.5 11.3 %all_gather.38 = bf16[1024,384]{1,0:T(8,128)(2,1)} all-gather(bf16[128,384]{1,0:T(8,128)(2,1)S(1)} %convolution_convert_fusion.2), channel_id=1, replica_groups=mesh['seq'=8,'head'=4] {'seq'}, dimensions={0}, use_global_device_ids=true | all-gather | bytes 884736 | tf_op jit(solution)/shard_map/all_gather | solution.py:79
  151.4 2.3 copy.33
  153.7 2.2 multiply_reduce_fusion.2
  156.5 9.2 %all_gather.42 = f32[1024,3]{0,1:T(4,128)} all-gather(f32[128,3]{0,1:T(4,128)S(1)} %get-tuple-element.6), channel_id=1, replica_groups=mesh['seq'=8,'head'=4] {'seq'}, dimensions={0}, use_global_device_ids=true | all-gather | bytes 13824 | tf_op jit(solution)/shard_map/all_gather | solution.py:137
  165.8 3.2 %multiply_reduce_fusion.1 = (f32[128,3]{0,1:T(4,128)}, f32[128,3,128]{0,2,1:T(8,128)}) fusion(f32[128,3,128]{0,2,1:T(8,128)S(1)} %bitcast.64, f32[128,3]{0,1:T(4,128)} %copy-done.12, f32[3,128]{1,0:T(4,128)} %bitcast.87, bf16[1024,3,128]{0,2,1:T(8,128)(2,1)S(1)} %bitcast.57, f32[3,128,1024]{2,1,0:T(8,128)S(1)} %get-tuple-element.5, ...), kind=kOutput, calls=%fused_computation.50 | convolution fusion | flops 203144832 | bytes 3644928 | tf_op jit(solution)/shard_map/hqk,khd->qhd/dot_general | solution.py:126
  172.0 10.1 %all_gather.39 = bf16[1024,384]{1,0:T(8,128)(2,1)S(1)} all-gather(bf16[128,384]{1,0:T(8,128)(2,1)S(1)} %fusion.32), channel_id=1, replica_groups=mesh['seq'=8,'head'=4] {'seq'}, dimensions={0}, use_global_device_ids=true | all-gather | bytes 884736 | tf_op jit(solution)/shard_map/all_gather | solution.py:130
  182.4 9.8 %all_gather.40 = f32[1024,3]{0,1:T(4,128)} all-gather(f32[128,3]{0,1:T(4,128)} %bitcast_add_fusion), channel_id=1, replica_groups=mesh['seq'=8,'head'=4] {'seq'}, dimensions={0}, use_global_device_ids=true | all-gather | bytes 13824 | tf_op jit(solution)/shard_map/all_gather | solution.py:136
  193.4 1.9 subtract_exponential_fusion
  196.3 3.3 %multiply_reduce_fusion = (f32[128,3]{0,1:T(4,128)}, f32[128,3,128]{0,2,1:T(8,128)}) fusion(f32[128,3,128]{0,2,1:T(8,128)S(1)} %bitcast.68, f32[128,3]{0,1:T(4,128)S(1)} %add_rsqrt_fusion, f32[3,128]{1,0:T(4,128)} %bitcast.84, bf16[1024,3,128]{0,2,1:T(8,128)(2,1)S(1)} %bitcast.59, f32[3,1024,128]{2,1,0:T(8,128)S(1)} %subtract_exponential_fusion, ...), kind=kOutput, calls=%fused_computation.46 | convolution fusion | flops 202702464 | bytes 3654144 | tf_op jit(solution)/shard_map/hqk,qhd->khd/dot_general | solution.py:147
  202.3 2.7 fusion.45
  208.6 2.2 convolution_convert_fusion
  210.8 41.5 %all-reduce.2.cloned.1.call-done = bf16[128,3072]{1,0:T(8,128)(2,1)} async-done(((bf16[128,3072]{1,0:T(8,128)(2,1)}), bf16[128,3072]{1,0:T(8,128)(2,1)}) %all-reduce.2.cloned.1.call-update) | async-done | bytes 786448 | tf_op jit(solution)/shard_map/psum | solution.py:168
  255.6 41.8 %reduce-scatter.2.cloned.1.call-done = bf16[384,384]{1,0:T(8,128)(2,1)} async-done(((bf16[3072,384]{1,0:T(8,128)(2,1)}), bf16[384,384]{1,0:T(8,128)(2,1)}) %reduce-scatter.2.cloned.1.call-update) | async-done | bytes 294928 | tf_op jit(solution)/shard_map/reduce_scatter | solution.py:104
  297.4 1.8 convert_element_type.124
  (97 shorter events, 26.6 us)
Async XLA Ops:
  7.2 2.9 copy-start
  7.2 3.4 %copy-start.16 = (f32[3072]{0:T(1024)S(1)}, f32[3072]{0:T(1024)}, u32[]{:S(2)}) copy-start(f32[3072]{0:T(1024)} %param.13) | copy-start | bytes 36868
  7.2 34.5 %copy-start.23 = (f32[3072]{0:T(1024)S(1)}, f32[3072]{0:T(1024)}, u32[]{:S(2)}) copy-start(f32[3072]{0:T(1024)} %param.14) | copy-start | bytes 36868
  7.2 34.5 %all-gather.5.cloned.1.call-start = ((), (), s32[]{:S(2)}) async-start(), calls=%async_computation.1 | async-start | bytes 2654208 | tf_op jit(solution)/shard_map/all_gather | solution.py:64
  7.9 64.7 %all-gather.7.cloned.1.call-start = ((), (), s32[]{:S(2)}) async-start(), calls=%async_computation.2 | async-start | bytes 2654208 | tf_op jit(solution)/shard_map/all_gather | solution.py:65
  8.7 95.0 %all-gather.9.cloned.1.call-start = ((), (), s32[]{:S(2)}) async-start(), calls=%async_computation.3 | async-start | bytes 2654208 | tf_op jit(solution)/shard_map/all_gather | solution.py:101
  9.4 126.1 %all-gather.11.cloned.1.call-start = ((), (), s32[]{:S(2)}) async-start(), calls=%async_computation.4 | async-start | bytes 2654208 | tf_op jit(solution)/shard_map/all_gather | solution.py:66
  10.0 242.3 %all-reduce.2.cloned.1.call-start = ((), (), s32[]{:S(2)}) async-start(), calls=%async_computation.5 | async-start | bytes 1572864 | tf_op jit(solution)/shard_map/psum | solution.py:168
  10.2 62.4 %copy-start.19 = (f32[128]{0:T(128)}, f32[128]{0:T(128)S(1)}, u32[]{:S(2)}) copy-start(f32[128]{0:T(128)S(1)} %broadcast_multiply_fusion.4) | copy-start | bytes 1540
  10.6 62.0 %copy-start.21 = (f32[128]{0:T(128)}, f32[128]{0:T(128)S(1)}, u32[]{:S(2)}) copy-start(f32[128]{0:T(128)S(1)} %add_rsqrt_fusion.2) | copy-start | bytes 1540
  44.0 28.6 %copy-start.8 = (f32[128,384]{1,0:T(8,128)}, f32[128,384]{1,0:T(8,128)S(1)}, u32[]{:S(2)}) copy-start(f32[128,384]{1,0:T(8,128)S(1)} %fusion.42) | copy-start | bytes 589828
  44.1 31.1 %copy-start.14 = (f32[384]{0:T(512)S(1)}, f32[384]{0:T(512)}, u32[]{:S(2)}) copy-start(f32[384]{0:T(512)} %param.21) | copy-start | bytes 4612
  75.2 28.4 %copy-start.4 = (bf16[128,3072]{1,0:T(8,128)(2,1)S(1)}, bf16[128,3072]{1,0:T(8,128)(2,1)}, u32[]{:S(2)}) copy-start(bf16[128,3072]{1,0:T(8,128)(2,1)} %param.12) | copy-start | bytes 2359300
  170.9 21.3 %copy-start.2 = (bf16[1024,384]{1,0:T(8,128)(2,1)S(1)}, bf16[1024,384]{1,0:T(8,128)(2,1)}, u32[]{:S(2)}) copy-start(bf16[1024,384]{1,0:T(8,128)(2,1)} %all_gather.41) | copy-start | bytes 2359300
  193.4 1.9 copy-start.1
  202.3 2.7 copy-start.7
  205.0 1.7 copy-start.6
  206.7 1.9 copy-start.5
  206.7 1.9 copy-start.11
  206.7 1.9 copy-start.13
  208.5 88.9 %reduce-scatter.2.cloned.1.call-start = ((), (), s32[]{:S(2)}) async-start(), calls=%async_computation.6 | async-start | bytes 2654208 | tf_op jit(solution)/shard_map/reduce_scatter | solution.py:104
  210.8 41.5 %copy-start.20 = (f32[128]{0:T(128)S(1)}, f32[128]{0:T(128)}, u32[]{:S(2)}) copy-start(f32[128]{0:T(128)} %copy-done.19) | copy-start | bytes 1540
  210.8 41.5 %copy-start.22 = (f32[128]{0:T(128)S(1)}, f32[128]{0:T(128)}, u32[]{:S(2)}) copy-start(f32[128]{0:T(128)} %copy-done.21) | copy-start | bytes 1540
  252.3 1.7 copy-start.3
  (6 other events, 4.6 us)
Sparse Core Ops, SparseCore 0:
  9.9 31.7 all-gather.4
  43.5 29.0 all-gather.6
  74.5 29.1 all-gather.8
  105.4 30.0 all-gather.10
  208.6 43.6 all-reduce.1
  255.5 41.8 reduce-scatter.1
where the time goes:
time: 307 us; the launch traced here: 306 us
  waiting for transfers between devices  174 us (57%)
  blocking collectives  64.9 us (21%)
  matrix products  29.7 us (10%)
  between operations  14.4 us (5%)
  other arithmetic  12.2 us (4%)
  local copies, waits for them, and re-layouts  10.8 us (4%)
    reduce_scatter x1, waiting for transfers between devices, body(): lax.psum_scatter(jnp.dot(columns.T, mix_flat, preferred_element_type=jnp....  41.8 us
    psum x1, waiting for transfers between devices, body(): lax.psum(partial_grad.astype(jnp.bfloat16), 'head').astype(jnp.float32)  41.5 us
    all_gather x1, waiting for transfers between devices, body(): lax.all_gather(query_weight, 'seq', axis=0, tiled=True)  31 us
    all_gather x1, waiting for transfers between devices, body(): lax.all_gather(key_weight, 'seq', axis=0, tiled=True)  28.5 us
    all_gather x1, waiting for transfers between devices, body(): lax.all_gather(output_weight, 'seq', axis=0, tiled=True)  17 us
    all_gather x1, blocking collectives, body(): lax.all_gather(mix_grad_flat.astype(jnp.float32), 'seq', axis=0, tiled=True)  13.3 us
    all_gather x1, waiting for transfers between devices, body(): lax.all_gather(value_weight, 'seq', axis=0, tiled=True)  11.5 us
    all_gather x1, blocking collectives, body(): lax.all_gather(values_flat, 'seq', axis=0, tiled=True)  11.3 us
  transfers between devices with their start and end apart: 6, of which 6 were waited for; matrix products, arithmetic and copies ran while one was open for 6% of the time, Pallas kernels for 0%

commit v1 on v0

v1 whole, which is shorter than its diff:
```python
import functools
import math

import jax
import jax.numpy as jnp
from jax import lax
from jax.experimental import pallas as pl
from jax.experimental.pallas import tpu as pltpu
from jax.sharding import PartitionSpec as P

HEAD_DIM = 128
EPSILON = 1e-06
F32 = jnp.float32
BF16 = jnp.bfloat16
K, V, Q, O = range(4)


def dot(a, b):
    return lax.dot_general(a, b, (((1,), (0,)), ((), ())), preferred_element_type=F32)


def dot_t(a, b):
    return lax.dot_general(a, b, (((1,), (1,)), ((), ())), preferred_element_type=F32)


def flipped(me, mask):
    out, bit = me, 0
    while (1 << bit) <= mask:
        if mask >> bit & 1:
            out = out + (1 << bit) * (1 - 2 * (lax.div(me, 1 << bit) % 2))
        bit += 1
    return out


def gather_orders(size):
    bits = [1 << b for b in range(size.bit_length() - 1)]
    return (bits[1:] + bits[:1], bits[1:][::-1] + bits[:1])


def scatter_orders(size):
    bits = [1 << b for b in range(size.bit_length() - 1)]
    return (bits[:1] + bits[1:], bits[:1] + bits[1:][::-1])


class Gather:
    def __init__(self, buf, index, me, size, send, recv):
        self.rows = buf.shape[2]
        self.copies = {}
        self.masks = sorted(range(1, size), key=lambda m: (bin(m).count("1"), m))
        self.orders = gather_orders(size)
        half = self.rows // 2
        for side, order in enumerate(self.orders):
            for mask in self.masks:
                last = [d for d in order if mask & d][-1]
                ref = buf.at[index, flipped(me, mask ^ last), pl.ds(side * half, half)]
                self.copies[side, mask] = pltpu.make_async_remote_copy(
                    src_ref=ref,
                    dst_ref=ref,
                    send_sem=send.at[index, side, mask],
                    recv_sem=recv.at[index, side, mask],
                    device_id={"seq": flipped(me, last)},
                    device_id_type=pl.DeviceIdType.MESH,
                )

    def push(self, side, mask):
        order = self.orders[side]
        start = 0
        for place, d in enumerate(order):
            if mask & d:
                start = place + 1
        for d in order[start:]:
            self.copies[side, mask | d].start()

    def begin(self):
        for side in range(2):
            self.push(side, 0)

    def proceed(self):
        for mask in self.masks:
            for side in range(2):
                self.copies[side, mask].wait_recv()
                self.push(side, mask)

    def finish(self):
        for copy in self.copies.values():
            copy.wait_send()


def kernel(
    seq,
    head,
    hidden_ref,
    cot_ref,
    scale_ref,
    shift_ref,
    gate_ref,
    qw_ref,
    kw_ref,
    vw_ref,
    ow_ref,
    qg_ref,
    kg_ref,
    grad_ref,
    outproj_ref,
    wall,
    act,
    stats,
    normed,
    cot,
    cot_t,
    expo,
    acc,
    rbuf,
    own,
    zs,
    zin,
    zmid,
    ztot,
    wsend,
    wrecv,
    asend,
    arecv,
    ssend,
    srecv,
    rsend,
    rrecv,
    zsend,
    zrecv,
):
    me = lax.axis_index("seq")
    hd = lax.axis_index("head")
    rows, width = hidden_ref.shape
    depth, cols = qw_ref.shape
    heads = cols // HEAD_DIM
    factor = F32(1.0 / math.sqrt(HEAD_DIM))
    mesh_ids = pl.DeviceIdType.MESH

    for index, ref in ((K, kw_ref), (V, vw_ref), (Q, qw_ref), (O, ow_ref)):
        wall[index, me] = ref[...]

    barrier = pltpu.get_barrier_semaphore()
    for step in range(1, seq):
        pl.semaphore_signal(
            barrier, inc=1, device_id={"seq": flipped(me, step)}, device_id_type=mesh_ids
        )
    for step in range(1, head):
        pl.semaphore_signal(
            barrier, inc=1, device_id={"head": (hd + step) % head}, device_id_type=mesh_ids
        )
    pl.semaphore_wait(barrier, seq - 1 + head - 1)

    weights = [Gather(wall, i, me, seq, wsend, wrecv) for i in range(4)]
    acts = [Gather(act, i, me, seq, asend, arecv) for i in range(4)]
    weights[K].begin()
    weights[V].begin()

    values = hidden_ref[...].astype(F32)
    center = values - jnp.mean(values, axis=-1, keepdims=True)
    mean = jnp.mean(values, axis=-1, keepdims=True)
    inverse = lax.rsqrt(jnp.mean(center * center, axis=-1, keepdims=True) + EPSILON)
    normed[...] = (center * inverse * (1.0 + scale_ref[...]) + shift_ref[...]).astype(BF16)
    branch = cot_ref[...].astype(F32) * gate_ref[...]
    cot[...] = branch.astype(BF16)
    cot_t[...] = jnp.transpose(branch).astype(BF16)

    def project(source, index):
        return dot(source[...], wall[index].reshape(width, cols))

    def head_norm(raw, gain_ref, scalar):
        units, inverses, outs = [], [], []
        for h in range(heads):
            part = raw[:, h * HEAD_DIM : (h + 1) * HEAD_DIM]
            inv = lax.rsqrt(jnp.mean(part * part, axis=-1, keepdims=True) + EPSILON)
            unit = part * inv
            gain = gain_ref[:, h * HEAD_DIM : (h + 1) * HEAD_DIM]
            units.append(unit)
            inverses.append(inv)
            outs.append((unit * gain * scalar).astype(BF16))
        return units, inverses, jnp.concatenate(outs, axis=1)

    def head_back(grad, unit, inv, gain, scalar):
        scaled = grad * gain * scalar
        along = jnp.mean(scaled * unit, axis=-1, keepdims=True)
        return (inv * (scaled - unit * along)).astype(BF16)

    weights[K].proceed()
    weights[Q].begin()
    key_unit, key_inverse, keys = head_norm(project(normed, K), kg_ref, F32(1.0))
    act[K, me] = keys
    acts[K].begin()
    weights[V].proceed()
    weights[O].begin()
    act[V, me] = project(normed, V).astype(BF16)
    acts[V].begin()
    weights[Q].proceed()
    query_unit, query_inverse, query = head_norm(project(normed, Q), qg_ref, factor)
    act[Q, me] = query
    acts[Q].begin()
    acts[K].proceed()
    acts[V].proceed()
    weights[O].proceed()
    act[O, me] = project(cot, O).astype(BF16)
    acts[O].begin()
    acts[Q].proceed()

    def lanes(h):
        return slice(h * HEAD_DIM, (h + 1) * HEAD_DIM)

    def whole(index, h):
        return act[index, :, :, lanes(h)].reshape(seq * rows, HEAD_DIM)

    lane = lax.broadcasted_iota(jnp.int32, (rows, rows), 1)
    table = jnp.zeros((rows, rows), F32)
    mixes, scales, deltas = [], [], []
    for h in range(heads):
        scores = dot_t(act[Q, me, :, lanes(h)], whole(K, h))
        top = jnp.max(scores, axis=-1, keepdims=True)
        part = jnp.exp(scores - top)
        total = jnp.sum(part, axis=-1, keepdims=True)
        expo[h] = part
        mix = (dot(part.astype(BF16), whole(V, h)) / total).astype(BF16)
        grad = act[O, me, :, lanes(h)]
        delta = jnp.sum(grad.astype(F32) * mix.astype(F32), axis=-1, keepdims=True)
        table = jnp.where(lane == h, top + jnp.log(total), table)
        table = jnp.where(lane == heads + h, delta, table)
        mixes.append(mix)
        scales.append(1.0 / total)
        deltas.append(delta)
    stats[me] = jnp.transpose(table)[: stats.shape[1]]
    sent = []
    for mask in range(1, seq):
        copy = pltpu.make_async_remote_copy(
            src_ref=stats.at[me],
            dst_ref=stats.at[me],
            send_sem=ssend.at[mask],
            recv_sem=srecv.at[mask],
            device_id={"seq": flipped(me, mask)},
            device_id_type=mesh_ids,
        )
        copy.start()
        sent.append(copy)

    mix_flat = jnp.concatenate(mixes, axis=1)
    for j in range(seq):
        acc[j] = dot(cot_t[j * depth : (j + 1) * depth, :], mix_flat).astype(BF16)

    half = depth // 2
    orders = scatter_orders(seq)
    moves = {}
    for side in range(2):
        for mask in range(1, seq):
            first = [d for d in orders[side] if mask & d][0]
            moves[side, mask] = pltpu.make_async_remote_copy(
                src_ref=acc.at[flipped(me, mask), pl.ds(side * half, half)],
                dst_ref=rbuf.at[mask, pl.ds(side * half, half)],
                send_sem=rsend.at[side, mask],
                recv_sem=rrecv.at[side, mask],
                device_id={"seq": flipped(me, first)},
                device_id_type=mesh_ids,
            )

    def stage(level):
        out = []
        for side in range(2):
            done = sum(orders[side][:level])
            d = orders[side][level]
            out += [(side, m, d) for m in range(1, seq) if m & d and not m & done]
        return out

    def scatter_send(level):
        for side, mask, _ in stage(level):
            moves[side, mask].start()

    def scatter_add(level):
        for side, mask, d in stage(level):
            moves[side, mask].wait_recv()
            span = pl.ds(side * half, half)
            slot = flipped(me, mask ^ d)
            total = acc[slot, span].astype(F32) + rbuf[mask, span].astype(F32)
            if mask == d and level == len(orders[0]) - 1:
                outproj_ref[span, :] = total
            else:
                acc[slot, span] = total.astype(BF16)

    scatter_send(0)
    acts[O].proceed()

    query_raw_grad, key_raw_grad, value_raw_grad = [], [], []
    for h in range(heads):
        prob_grad = dot_t(act[O, me, :, lanes(h)], whole(V, h))
        score_grad = (expo[h] * scales[h] * (prob_grad - deltas[h])).astype(BF16)
        query_grad = dot(score_grad, whole(K, h))
        query_raw_grad.append(
            head_back(query_grad, query_unit[h], query_inverse[h], qg_ref[:, lanes(h)], factor)
        )
    scatter_add(0)
    if len(orders[0]) > 1:
        scatter_send(1)

    for copy in sent:
        copy.wait_recv()
    for h in range(heads):
        log_row = jnp.concatenate([stats[j, h : h + 1, :] for j in range(seq)], axis=1)
        delta_row = jnp.concatenate(
            [stats[j, heads + h : heads + h + 1, :] for j in range(seq)], axis=1
        )
        probs = jnp.exp(dot_t(act[K, me, :, lanes(h)], whole(Q, h)) - log_row)
        prob_grad = dot_t(act[V, me, :, lanes(h)], whole(O, h))
        score_grad = (probs * (prob_grad - delta_row)).astype(BF16)
        key_grad = dot(score_grad, whole(Q, h))
        value_raw_grad.append(dot(probs.astype(BF16), whole(O, h)).astype(BF16))
        key_raw_grad.append(
            head_back(key_grad, key_unit[h], key_inverse[h], kg_ref[:, lanes(h)], F32(1.0))
        )
    query_raw_grad = jnp.concatenate(query_raw_grad, axis=1)
    key_raw_grad = jnp.concatenate(key_raw_grad, axis=1)
    value_raw_grad = jnp.concatenate(value_raw_grad, axis=1)

    chunks, _, chunk = zs.shape
    per = chunk // depth
    mid = head // 2
    left = hd < mid
    inward = jnp.where(left, hd + 1, hd - 1)
    outward = jnp.where(left, hd - 1, hd + 1)
    place = jnp.where(left, hd, head - 1 - hd)
    inner = place == mid - 1

    def zcopy(src, dst, kind, c, target):
        return pltpu.make_async_remote_copy(
            src_ref=src.at[c],
            dst_ref=dst.at[c],
            send_sem=zsend.at[kind, c],
            recv_sem=zrecv.at[kind, c],
            device_id={"head": target},
            device_id_type=mesh_ids,
        )

    to_next = [zcopy(zs, zin, 0, c, inward) for c in range(chunks)]
    to_mid = [zcopy(zs, zmid, 1, c, inward) for c in range(chunks)]
    to_out = [zcopy(ztot, ztot, 2, c, outward) for c in range(chunks)]

    for c in range(chunks):
        def part(index, c=c):
            return wall[index, c * per : (c + 1) * per].reshape(chunk, cols)

        grad = dot_t(query_raw_grad, part(Q))
        grad = grad + dot_t(key_raw_grad, part(K))
        grad = grad + dot_t(value_raw_grad, part(V))
        own[c] = grad

        @pl.when(place == 0)
        def _(c=c):
            zs[c] = own[c].astype(BF16)
            if mid > 1:
                to_next[c].start()
            else:
                to_mid[c].start()

    lag = 2
    for level in range(1, len(orders[0])):
        if level > 1:
            scatter_send(level)
        if level < len(orders[0]) - 1:
            scatter_add(level)

    for c in range(chunks + lag):
        if c < chunks and mid > 1:

            @pl.when(place > 0)
            def _(c=c):
                to_next[c].wait_recv()
                zs[c] = (own[c] + zin[c].astype(F32)).astype(BF16)

                @pl.when(inner)
                def _():
                    to_mid[c].start()

                @pl.when(jnp.logical_not(inner))
                def _():
                    to_next[c].start()

        if c >= lag:
            b = c - lag

            @pl.when(inner)
            def _(b=b):
                to_mid[b].wait_recv()
                ztot[b] = (zs[b].astype(F32) + zmid[b].astype(F32)).astype(BF16)

            @pl.when(jnp.logical_not(inner))
            def _(b=b):
                to_out[b].wait_recv()

            @pl.when(place > 0)
            def _(b=b):
                to_out[b].start()

    scatter_add(len(orders[0]) - 1)

    middle = jnp.zeros((rows, 1), F32)
    along = jnp.zeros((rows, 1), F32)

    def pieces(c):
        span = slice(c * chunk, (c + 1) * chunk)
        unit = (hidden_ref[:, span].astype(F32) - mean) * inverse
        return span, unit, ztot[c].astype(F32) * (1.0 + scale_ref[:, span])

    for c in range(chunks):
        _, unit, scaled = pieces(c)
        middle = middle + jnp.sum(scaled, axis=-1, keepdims=True)
        along = along + jnp.sum(scaled * unit, axis=-1, keepdims=True)
    middle = middle / width
    along = along / width
    for c in range(chunks):
        span, unit, scaled = pieces(c)
        grad_ref[:, span] = (inverse * (scaled - middle - unit * along)).astype(BF16)

    for gather in weights + acts:
        gather.finish()
    for copy in sent:
        copy.wait_send()
    for copy in moves.values():
        copy.wait_send()
    for c in range(chunks):
        if mid > 1:

            @pl.when(jnp.logical_not(inner))
            def _(c=c):
                to_next[c].wait_send()

        @pl.when(inner)
        def _(c=c):
            to_mid[c].wait_send()

        @pl.when(place > 0)
        def _(c=c):
            to_out[c].wait_send()


def body(seq, head, *args):
    hidden, cotangent, mod_scale, mod_shift, branch_gate, qw, kw, vw, ow, qg, kg = args
    rows, width = hidden.shape
    depth, cols = qw.shape
    heads = cols // HEAD_DIM
    chunk = math.lcm(depth, 128)
    chunks = width // chunk
    stat_rows = -(-2 * heads // 8) * 8
    vmem = pl.BlockSpec(memory_space=pltpu.VMEM)
    dma = pltpu.SemaphoreType.DMA
    zshape = (chunks, rows, chunk)
    return tuple(
        pl.pallas_call(
            functools.partial(kernel, seq, head),
            out_shape=(
                jax.ShapeDtypeStruct((rows, width), BF16),
                jax.ShapeDtypeStruct((depth, cols), F32),
            ),
            in_specs=[vmem] * 11,
            out_specs=(vmem, vmem),
            scratch_shapes=[
                pltpu.VMEM((4, seq, depth, cols), BF16),
                pltpu.VMEM((4, seq, rows, cols), BF16),
                pltpu.VMEM((seq, stat_rows, rows), F32),
                pltpu.VMEM((rows, width), BF16),
                pltpu.VMEM((rows, width), BF16),
                pltpu.VMEM((width, rows), BF16),
                pltpu.VMEM((heads, rows, seq * rows), F32),
                pltpu.VMEM((seq, depth, cols), BF16),
                pltpu.VMEM((seq, depth, cols), BF16),
                pltpu.VMEM(zshape, F32),
                pltpu.VMEM(zshape, BF16),
                pltpu.VMEM(zshape, BF16),
                pltpu.VMEM(zshape, BF16),
                pltpu.VMEM(zshape, BF16),
                dma((4, 2, seq)),
                dma((4, 2, seq)),
                dma((4, 2, seq)),
                dma((4, 2, seq)),
                dma((seq,)),
                dma((seq,)),
                dma((2, seq)),
                dma((2, seq)),
                dma((3, chunks)),
                dma((3, chunks)),
            ],
            compiler_params=pltpu.CompilerParams(
                collective_id=0, has_side_effects=True, vmem_limit_bytes=56 * 1024 * 1024
            ),
        )(
            hidden,
            cotangent,
            mod_scale.reshape(1, -1),
            mod_shift.reshape(1, -1),
            branch_gate.reshape(1, -1),
            qw,
            kw,
            vw,
            ow,
            qg.reshape(1, -1),
            kg.reshape(1, -1),
        )
    )


def solution(mesh):
    placed = (
        P("seq", None),
        P("seq", None),
        P(),
        P(),
        P(),
        P("seq", "head"),
        P("seq", "head"),
        P("seq", "head"),
        P("seq", "head"),
        P("head"),
        P("head"),
    )
    return jax.shard_map(
        functools.partial(body, mesh.shape["seq"], mesh.shape["head"]),
        mesh=mesh,
        in_specs=placed,
        out_specs=(P("seq", None), P("seq", "head")),
        check_vma=False,
    )
```

time: 307 us -> 131 us (0.43)
  waiting for transfers between devices: 174 us -> 0 us
  Pallas kernels: 0 us -> 125 us
  blocking collectives: 64.9 us -> 0 us
  matrix products: 29.7 us -> 0 us
  between operations: 14.4 us -> 0.66 us
  other arithmetic: 12.2 us -> 0 us
  local copies, waits for them, and re-layouts: 10.8 us -> 4.86 us
    pallas_call x0 -> x1, Pallas kernels: none -> 125 us  [body(): pl.pallas_call(functools.partial(kernel, seq, head), out_shape=(jax.Shape...]
    all_gather x4 -> x0, waiting for transfers between devices: 88 us -> none  [the longest x1 31 us: body(): lax.all_gather(query_weight, 'seq', axis=0, tiled=True)]
    all_gather x6 -> x0, blocking collectives: 64.9 us -> none  [the longest x1 13.3 us: body(): lax.all_gather(mix_grad_flat.astype(jnp.float32), 'seq', axis=0, tiled=True)]
    reduce_scatter x1 -> x0, waiting for transfers between devices: 41.8 us -> none  [body(): lax.psum_scatter(jnp.dot(columns.T, mix_flat, preferred_element_type=jnp....]
    psum x1 -> x0, waiting for transfers between devices: 41.5 us -> none  [body(): lax.psum(partial_grad.astype(jnp.bfloat16), 'head').astype(jnp.float32)]
    dot_general x14 -> x0, matrix products: 29.7 us -> none  [the longest x3 6.91 us: body(): jnp.dot(columns, piece, preferred_element_type=jnp.float32)]
    convert_element_type x6 -> x0, other arithmetic: 6.35 us -> none  [the longest x2 1.93 us: head_back(): return (inverse * (scaled - unit * along)).astype(jnp.bfloat16)]
    convert_element_type x4 -> x0, local copies, waits for them, and re-layouts: 3.83 us -> none  [the longest x1 1.63 us: body(): values = value_raw.reshape(cube).astype(jnp.bfloat16)]
  transfers between devices with their start and end apart: 6 -> 0, of which waited for: 6 -> 0; matrix products, arithmetic and copies ran while one was open for 6% -> 0% of each run, Pallas kernels for 0% -> 0%
where the time goes in v1:
time: 131 us; the launch traced here: 130 us
  Pallas kernels  125 us (95%)
  local copies, waits for them, and re-layouts  4.86 us (4%)
    pallas_call x1, Pallas kernels, body(): pl.pallas_call(functools.partial(kernel, seq, head), out_shape=(jax.Shape...  125 us
    unnamed x8, local copies, waits for them, and re-layouts  3.74 us

profile of v1, /device:TPU:0, one launch (start us, length us, event | category | flops | bytes accessed | tf_op | source)
XLA Modules:
  0.0 130.3 jit_solution(6541123922535599772)
XLA Ops:
  0.6 0.0 copy-start.1
  0.6 0.7 copy-done.1
  1.3 0.0 copy-start.2
  1.3 0.6 reshape.22.qg_ref
  1.9 0.1 copy-done.2
  2.0 0.6 reshape.23.kg_ref
  2.6 124.8 %shard_map.122 = (bf16[128,3072]{1,0:T(8,128)(2,1)}, f32[384,384]{1,0:T(8,128)}) custom-call(bf16[128,3072]{1,0:T(8,128)(2,1)} %hidden_ref.1, bf16[128,3072]{1,0:T(8,128)(2,1)} %cot_ref.1, f32[1,3072]{1,0:T(1,128)} %bitcast.3, f32[1,3072]{1,0:T(1,128)} %bitcast.4, f32[1,3072]{1,0:T(1,128)} %bitcast.5, bf16[384,384]{1,0:T(8,128)(2,1)} %qw_ref.1, ...), custom_call_target="tpu_custom_call" | custom-call | tf_op jit(solution)/shard_map/pallas_call | solution.py:452
  127.3 0.0 copy-start
  127.4 2.1 %copy.15 = bf16[128,3072]{1,0:T(8,128)(2,1)} copy(bf16[128,3072]{1,0:T(8,128)(2,1)} %get-tuple-element.4) | data formatting | bytes 1572864
  129.5 0.0 copy-done
  129.5 0.8 copy.16
Async XLA Ops:
  0.6 0.7 copy-start.1
  1.3 0.7 copy-start.2
  127.3 2.1 %copy-start = (f32[384,384]{1,0:T(8,128)S(1)}, f32[384,384]{1,0:T(8,128)}, u32[]{:S(2)}) copy-start(f32[384,384]{1,0:T(8,128)} %get-tuple-element.5) | copy-start | bytes 1769476

commit v2 on v1

--- a/solution.py
+++ b/solution.py
@@ -75,8 +75,10 @@
         for side in range(2):
             self.push(side, 0)
 
-    def proceed(self):
+    def proceed(self, low=1, high=99):
         for mask in self.masks:
+            if not low <= bin(mask).count("1") <= high:
+                continue
             for side in range(2):
                 self.copies[side, mask].wait_recv()
                 self.push(side, mask)
@@ -89,8 +91,8 @@
 def kernel(
     seq,
     head,
-    hidden_ref,
-    cot_ref,
+    hidden_hbm,
+    cot_hbm,
     scale_ref,
     shift_ref,
     gate_ref,
@@ -100,8 +102,11 @@
     ow_ref,
     qg_ref,
     kg_ref,
-    grad_ref,
+    sum_ref,
+    rowstat_ref,
     outproj_ref,
+    hidden_ref,
+    cot_ref,
     wall,
     act,
     stats,
@@ -126,6 +131,7 @@
     rrecv,
     zsend,
     zrecv,
+    load,
 ):
     me = lax.axis_index("seq")
     hd = lax.axis_index("head")
@@ -135,8 +141,14 @@
     factor = F32(1.0 / math.sqrt(HEAD_DIM))
     mesh_ids = pl.DeviceIdType.MESH
 
-    for index, ref in ((K, kw_ref), (V, vw_ref), (Q, qw_ref), (O, ow_ref)):
-        wall[index, me] = ref[...]
+    loads = [
+        pltpu.make_async_copy(ref, wall.at[index, me], load.at[index])
+        for index, ref in ((K, kw_ref), (V, vw_ref), (Q, qw_ref), (O, ow_ref))
+    ]
+    loads.insert(2, pltpu.make_async_copy(hidden_hbm, hidden_ref, load.at[4]))
+    loads.append(pltpu.make_async_copy(cot_hbm, cot_ref, load.at[5]))
+    for copy in loads:
+        copy.start()
 
     barrier = pltpu.get_barrier_semaphore()
     for step in range(1, seq):
@@ -151,17 +163,21 @@
 
     weights = [Gather(wall, i, me, seq, wsend, wrecv) for i in range(4)]
     acts = [Gather(act, i, me, seq, asend, arecv) for i in range(4)]
+    loads[0].wait()
     weights[K].begin()
+    loads[1].wait()
     weights[V].begin()
+    for copy in loads[2:]:
+        copy.wait()
 
     values = hidden_ref[...].astype(F32)
     center = values - jnp.mean(values, axis=-1, keepdims=True)
     mean = jnp.mean(values, axis=-1, keepdims=True)
     inverse = lax.rsqrt(jnp.mean(center * center, axis=-1, keepdims=True) + EPSILON)
     normed[...] = (center * inverse * (1.0 + scale_ref[...]) + shift_ref[...]).astype(BF16)
-    branch = cot_ref[...].astype(F32) * gate_ref[...]
-    cot[...] = branch.astype(BF16)
-    cot_t[...] = jnp.transpose(branch).astype(BF16)
+
+    def lanes(h):
+        return slice(h * HEAD_DIM, (h + 1) * HEAD_DIM)
 
     def project(source, index):
         return dot(source[...], wall[index].reshape(width, cols))
@@ -172,7 +188,7 @@
             part = raw[:, h * HEAD_DIM : (h + 1) * HEAD_DIM]
             inv = lax.rsqrt(jnp.mean(part * part, axis=-1, keepdims=True) + EPSILON)
             unit = part * inv
-            gain = gain_ref[:, h * HEAD_DIM : (h + 1) * HEAD_DIM]
+            gain = gain_ref[lanes(h)][None, :]
             units.append(unit)
             inverses.append(inv)
             outs.append((unit * gain * scalar).astype(BF16))
@@ -188,6 +204,9 @@
     key_unit, key_inverse, keys = head_norm(project(normed, K), kg_ref, F32(1.0))
     act[K, me] = keys
     acts[K].begin()
+    branch = cot_ref[...].astype(F32) * gate_ref[...]
+    cot[...] = branch.astype(BF16)
+    cot_t[...] = jnp.transpose(branch).astype(BF16)
     weights[V].proceed()
     weights[O].begin()
     act[V, me] = project(normed, V).astype(BF16)
@@ -196,15 +215,15 @@
     query_unit, query_inverse, query = head_norm(project(normed, Q), qg_ref, factor)
     act[Q, me] = query
     acts[Q].begin()
-    acts[K].proceed()
-    acts[V].proceed()
-    weights[O].proceed()
+    weights[O].proceed(1, 1)
+    acts[K].proceed(1, 1)
+    acts[V].proceed(1, 1)
+    weights[O].proceed(2)
     act[O, me] = project(cot, O).astype(BF16)
     acts[O].begin()
-    acts[Q].proceed()
-
-    def lanes(h):
-        return slice(h * HEAD_DIM, (h + 1) * HEAD_DIM)
+    acts[K].proceed(2)
+    acts[Q].proceed(1, 1)
+    acts[V].proceed(2)
 
     def whole(index, h):
         return act[index, :, :, lanes(h)].reshape(seq * rows, HEAD_DIM)
@@ -226,6 +245,11 @@
         mixes.append(mix)
         scales.append(1.0 / total)
         deltas.append(delta)
+        if h == 0:
+            acts[O].proceed(1, 1)
+            acts[Q].proceed(2, 2)
+        if h == min(1, heads - 1):
+            acts[O].proceed(2, 2)
     stats[me] = jnp.transpose(table)[: stats.shape[1]]
     sent = []
     for mask in range(1, seq):
@@ -241,9 +265,6 @@
         sent.append(copy)
 
     mix_flat = jnp.concatenate(mixes, axis=1)
-    for j in range(seq):
-        acc[j] = dot(cot_t[j * depth : (j + 1) * depth, :], mix_flat).astype(BF16)
-
     half = depth // 2
     orders = scatter_orders(seq)
     moves = {}
@@ -282,21 +303,16 @@
             else:
                 acc[slot, span] = total.astype(BF16)
 
-    scatter_send(0)
-    acts[O].proceed()
-
     query_raw_grad, key_raw_grad, value_raw_grad = [], [], []
     for h in range(heads):
         prob_grad = dot_t(act[O, me, :, lanes(h)], whole(V, h))
         score_grad = (expo[h] * scales[h] * (prob_grad - deltas[h])).astype(BF16)
         query_grad = dot(score_grad, whole(K, h))
         query_raw_grad.append(
-            head_back(query_grad, query_unit[h], query_inverse[h], qg_ref[:, lanes(h)], factor)
-        )
-    scatter_add(0)
-    if len(orders[0]) > 1:
-        scatter_send(1)
-
+            head_back(query_grad, query_unit[h], query_inverse[h], qg_ref[lanes(h)][None, :], factor)
+        )
+    acts[Q].proceed(3)
+    acts[O].proceed(3)
     for copy in sent:
         copy.wait_recv()
     for h in range(heads):
@@ -310,13 +326,15 @@
         key_grad = dot(score_grad, whole(Q, h))
         value_raw_grad.append(dot(probs.astype(BF16), whole(O, h)).astype(BF16))
         key_raw_grad.append(
-            head_back(key_grad, key_unit[h], key_inverse[h], kg_ref[:, lanes(h)], F32(1.0))
+            head_back(key_grad, key_unit[h], key_inverse[h], kg_ref[lanes(h)][None, :], F32(1.0))
         )
     query_raw_grad = jnp.concatenate(query_raw_grad, axis=1)
     key_raw_grad = jnp.concatenate(key_raw_grad, axis=1)
     value_raw_grad = jnp.concatenate(value_raw_grad, axis=1)
 
-    chunks, _, chunk = zs.shape
+    messages, split, chunk = zs.shape
+    parts = rows // split
+    chunks = messages // parts
     per = chunk // depth
     mid = head // 2
     left = hd < mid
@@ -335,85 +353,102 @@
             device_id_type=mesh_ids,
         )
 
-    to_next = [zcopy(zs, zin, 0, c, inward) for c in range(chunks)]
-    to_mid = [zcopy(zs, zmid, 1, c, inward) for c in range(chunks)]
-    to_out = [zcopy(ztot, ztot, 2, c, outward) for c in range(chunks)]
-
-    for c in range(chunks):
-        def part(index, c=c):
+    to_next = [zcopy(zs, zin, 0, c, inward) for c in range(messages)]
+    to_mid = [zcopy(zs, zmid, 1, c, inward) for c in range(messages)]
+    to_out = [zcopy(ztot, ztot, 2, c, outward) for c in range(messages)]
+
+    def own_part(c):
+        def part(index):
             return wall[index, c * per : (c + 1) * per].reshape(chunk, cols)
 
         grad = dot_t(query_raw_grad, part(Q))
         grad = grad + dot_t(key_raw_grad, part(K))
         grad = grad + dot_t(value_raw_grad, part(V))
-        own[c] = grad
+        for p in range(parts):
+            own[c * parts + p] = grad[p * split : (p + 1) * split]
 
         @pl.when(place == 0)
-        def _(c=c):
-            zs[c] = own[c].astype(BF16)
-            if mid > 1:
-                to_next[c].start()
-            else:
-                to_mid[c].start()
-
-    lag = 2
-    for level in range(1, len(orders[0])):
-        if level > 1:
+        def _():
+            for b in range(c * parts, (c + 1) * parts):
+                zs[b] = own[b].astype(BF16)
+                if mid > 1:
+                    to_next[b].start()
+                else:
+                    to_mid[b].start()
+
+    def pass_in(b):
+        @pl.when(place > 0)
+        def _():
+            to_next[b].wait_recv()
+            zs[b] = (own[b] + zin[b].astype(F32)).astype(BF16)
+
+            @pl.when(inner)
+            def _():
+                to_mid[b].start()
+
+            @pl.when(jnp.logical_not(inner))
+            def _():
+                to_next[b].start()
+
+    middle = [jnp.zeros((split, 1), F32)] * parts
+    along = [jnp.zeros((split, 1), F32)] * parts
+
+    def pass_out(b):
+        @pl.when(inner)
+        def _():
+            to_mid[b].wait_recv()
+            ztot[b] = (zs[b].astype(F32) + zmid[b].astype(F32)).astype(BF16)
+
+        @pl.when(jnp.logical_not(inner))
+        def _():
+            to_out[b].wait_recv()
+
+        @pl.when(place > 0)
+        def _():
+            to_out[b].start()
+
+        c, p = b // parts, b % parts
+        span = slice(c * chunk, (c + 1) * chunk)
+        tokens = slice(p * split, (p + 1) * split)
+        unit = (hidden_ref[tokens, span].astype(F32) - mean[tokens]) * inverse[tokens]
+        total = ztot[b]
+        sum_ref[tokens, span] = total
+        scaled = total.astype(F32) * (1.0 + scale_ref[:, span])
+        middle[p] = middle[p] + jnp.sum(scaled, axis=-1, keepdims=True)
+        along[p] = along[p] + jnp.sum(scaled * unit, axis=-1, keepdims=True)
+
+    levels = len(orders[0])
+    early = max(chunks // 2, 1)
+    share = -(-seq // early)
+    for c in range(chunks + 3):
+        if c < chunks:
+            own_part(c)
+        for j in range(c * share, min((c + 1) * share, seq)):
+            acc[j] = dot(cot_t[j * depth : (j + 1) * depth, :], mix_flat).astype(BF16)
+        if c == early - 1:
+            scatter_send(0)
+        for p in range(parts):
+            if 1 <= c <= chunks and mid > 1:
+                pass_in((c - 1) * parts + p)
+            if c >= 3:
+                pass_out((c - 3) * parts + p)
+        if c == early + 1:
+            scatter_add(0)
+            if levels > 1:
+                scatter_send(1)
+        if c == chunks and levels > 2:
+            scatter_add(1)
+            scatter_send(2)
+    for level in range(min(levels - 1, 2), levels):
+        if level > 2:
             scatter_send(level)
-        if level < len(orders[0]) - 1:
+        if level > 0:
             scatter_add(level)
 
-    for c in range(chunks + lag):
-        if c < chunks and mid > 1:
-
-            @pl.when(place > 0)
-            def _(c=c):
-                to_next[c].wait_recv()
-                zs[c] = (own[c] + zin[c].astype(F32)).astype(BF16)
-
-                @pl.when(inner)
-                def _():
-                    to_mid[c].start()
-
-                @pl.when(jnp.logical_not(inner))
-                def _():
-                    to_next[c].start()
-
-        if c >= lag:
-            b = c - lag
-
-            @pl.when(inner)
-            def _(b=b):
-                to_mid[b].wait_recv()
-                ztot[b] = (zs[b].astype(F32) + zmid[b].astype(F32)).astype(BF16)
-
-            @pl.when(jnp.logical_not(inner))
-            def _(b=b):
-                to_out[b].wait_recv()
-
-            @pl.when(place > 0)
-            def _(b=b):
-                to_out[b].start()
-
-    scatter_add(len(orders[0]) - 1)
-
-    middle = jnp.zeros((rows, 1), F32)
-    along = jnp.zeros((rows, 1), F32)
-
-    def pieces(c):
-        span = slice(c * chunk, (c + 1) * chunk)
-        unit = (hidden_ref[:, span].astype(F32) - mean) * inverse
-        return span, unit, ztot[c].astype(F32) * (1.0 + scale_ref[:, span])
-
-    for c in range(chunks):
-        _, unit, scaled = pieces(c)
-        middle = middle + jnp.sum(scaled, axis=-1, keepdims=True)
-        along = along + jnp.sum(scaled * unit, axis=-1, keepdims=True)
-    middle = middle / width
-    along = along / width
-    for c in range(chunks):
-        span, unit, scaled = pieces(c)
-        grad_ref[:, span] = (inverse * (scaled - middle - unit * along)).astype(BF16)
+    column = lax.broadcasted_iota(jnp.int32, (rows, 128), 1)
+    rowstat = jnp.where(column == 0, mean, inverse)
+    rowstat = jnp.where(column == 2, jnp.concatenate(middle, axis=0) / width, rowstat)
+    rowstat_ref[...] = jnp.where(column == 3, jnp.concatenate(along, axis=0) / width, rowstat)
 
     for gather in weights + acts:
         gather.finish()
@@ -421,7 +456,7 @@
         copy.wait_send()
     for copy in moves.values():
         copy.wait_send()
-    for c in range(chunks):
+    for c in range(messages):
         if mid > 1:
 
             @pl.when(jnp.logical_not(inner))
@@ -435,6 +470,14 @@
         @pl.when(place > 0)
         def _(c=c):
             to_out[c].wait_send()
+
+
+def finish(hidden_ref, total_ref, scale_ref, rowstat_ref, outproj_ref, grad_ref, out_ref):
+    mean, inverse, middle, along = (rowstat_ref[:, i : i + 1] for i in range(4))
+    unit = (hidden_ref[...].astype(F32) - mean) * inverse
+    scaled = total_ref[...].astype(F32) * (1.0 + scale_ref[...])
+    grad_ref[...] = (inverse * (scaled - middle - unit * along)).astype(BF16)
+    out_ref[...] = outproj_ref[...]
 
 
 def body(seq, head, *args):
@@ -447,17 +490,22 @@
     stat_rows = -(-2 * heads // 8) * 8
     vmem = pl.BlockSpec(memory_space=pltpu.VMEM)
     dma = pltpu.SemaphoreType.DMA
-    zshape = (chunks, rows, chunk)
-    return tuple(
+    parts = 2 if rows % 32 == 0 else 1
+    zshape = (chunks * parts, rows // parts, chunk)
+    anywhere = pl.BlockSpec(memory_space=pl.ANY)
+    total, rowstat, outproj = (
         pl.pallas_call(
             functools.partial(kernel, seq, head),
             out_shape=(
                 jax.ShapeDtypeStruct((rows, width), BF16),
+                jax.ShapeDtypeStruct((rows, 128), F32),
                 jax.ShapeDtypeStruct((depth, cols), F32),
             ),
-            in_specs=[vmem] * 11,
-            out_specs=(vmem, vmem),
+            in_specs=[anywhere] * 2 + [vmem] * 3 + [anywhere] * 4 + [vmem] * 2,
+            out_specs=(vmem, vmem, vmem),
             scratch_shapes=[
+                pltpu.VMEM((rows, width), BF16),
+                pltpu.VMEM((rows, width), BF16),
                 pltpu.VMEM((4, seq, depth, cols), BF16),
                 pltpu.VMEM((4, seq, rows, cols), BF16),
                 pltpu.VMEM((seq, stat_rows, rows), F32),
@@ -480,8 +528,9 @@
                 dma((seq,)),
                 dma((2, seq)),
                 dma((2, seq)),
-                dma((3, chunks)),
-                dma((3, chunks)),
+                dma((3, chunks * parts)),
+                dma((3, chunks * parts)),
+                dma((6,)),
             ],
             compiler_params=pltpu.CompilerParams(
                 collective_id=0, has_side_effects=True, vmem_limit_bytes=56 * 1024 * 1024
@@ -496,9 +545,31 @@
             kw,
             vw,
             ow,
-            qg.reshape(1, -1),
-            kg.reshape(1, -1),
-        )
+            qg,
+            kg,
+        )
+    )
+    steps = 4 if width % 512 == 0 and depth % 32 == 0 else 1
+    across = pl.BlockSpec((rows, width // steps), lambda i: (0, i))
+    down = pl.BlockSpec((depth // steps, cols), lambda i: (i, 0))
+    return tuple(
+        pl.pallas_call(
+            finish,
+            grid=(steps,),
+            out_shape=(
+                jax.ShapeDtypeStruct((rows, width), BF16),
+                jax.ShapeDtypeStruct((depth, cols), F32),
+            ),
+            in_specs=[
+                across,
+                across,
+                pl.BlockSpec((1, width // steps), lambda i: (0, i)),
+                pl.BlockSpec((rows, 128), lambda i: (0, 0)),
+                down,
+            ],
+            out_specs=(across, down),
+            compiler_params=pltpu.CompilerParams(vmem_limit_bytes=56 * 1024 * 1024),
+        )(hidden, total, mod_scale.reshape(1, -1), rowstat, outproj)
     )
 
 

time: 131 us -> 121 us (0.924)
  Pallas kernels: 125 us -> 120 us
  local copies, waits for them, and re-layouts: 4.86 us -> 0 us
    pallas_call x1, Pallas kernels: 125 us -> 116 us  [body(): pl.pallas_call(functools.partial(kernel, seq, head), out_shape=(jax.Shape...]
    pallas_call x0 -> x1, Pallas kernels: none -> 4.16 us  [body(): pl.pallas_call(finish, grid=(steps,), out_shape=(jax.ShapeDtypeStruct((ro...]
    unnamed x8 -> x0, local copies, waits for them, and re-layouts: 3.74 us -> none
where the time goes in v2:
time: 121 us
  Pallas kernels  120 us (99%)
    pallas_call x1, Pallas kernels, body(): pl.pallas_call(functools.partial(kernel, seq, head), out_shape=(jax.Shape...  116 us
    pallas_call x1, Pallas kernels, body(): pl.pallas_call(finish, grid=(steps,), out_shape=(jax.ShapeDtypeStruct((ro...  4.16 us

profile of v2, /device:TPU:0, one launch (start us, length us, event | category | flops | bytes accessed | tf_op | source)
XLA Modules:
  0.0 120.9 jit_solution(3369209896872542899)
XLA Ops:
  0.6 116.1 %shard_map.122 = (bf16[128,3072]{1,0:T(8,128)(2,1)}, f32[128,128]{1,0:T(8,128)}, f32[384,384]{1,0:T(8,128)}) custom-call(bf16[128,3072]{1,0:T(8,128)(2,1)} %hidden_ref.1, bf16[128,3072]{1,0:T(8,128)(2,1)} %cot_hbm.1, f32[1,3072]{1,0:T(1,128)} %bitcast.3, f32[1,3072]{1,0:T(1,128)} %bitcast.5, f32[1,3072]{1,0:T(1,128)} %bitcast.6, bf16[384,384]{1,0:T(8,128)(2,1)} %qw_ref.1, ...), custom_call_target="tpu_custom_call" | custom-call | tf_op jit(solution)/shard_map/pallas_call | solution.py:497
  116.7 4.2 %shard_map.123 = (bf16[128,3072]{1,0:T(8,128)(2,1)}, f32[384,384]{1,0:T(8,128)}) custom-call(bf16[128,3072]{1,0:T(8,128)(2,1)} %hidden_ref.1, bf16[128,3072]{1,0:T(8,128)(2,1)} %get-tuple-element.5.total_ref, f32[1,3072]{1,0:T(1,128)} %bitcast.4, f32[128,128]{1,0:T(8,128)} %get-tuple-element.6.rowstat_ref, f32[384,384]{1,0:T(8,128)} %get-tuple-element.7.outproj_ref), custom_call_target="tpu_custom_call" | custom-call | tf_op jit(solution)/shard_map/pallas_call | solution.py:556

commit v3 on v2

--- a/solution.py
+++ b/solution.py
@@ -208,21 +208,17 @@
     cot[...] = branch.astype(BF16)
     cot_t[...] = jnp.transpose(branch).astype(BF16)
     weights[V].proceed()
-    weights[O].begin()
     act[V, me] = project(normed, V).astype(BF16)
     acts[V].begin()
-    weights[Q].proceed()
+    weights[Q].proceed(1, 1)
+    acts[K].proceed(1, 1)
+    weights[O].begin()
+    weights[Q].proceed(2)
     query_unit, query_inverse, query = head_norm(project(normed, Q), qg_ref, factor)
     act[Q, me] = query
     acts[Q].begin()
-    weights[O].proceed(1, 1)
-    acts[K].proceed(1, 1)
     acts[V].proceed(1, 1)
-    weights[O].proceed(2)
-    act[O, me] = project(cot, O).astype(BF16)
-    acts[O].begin()
     acts[K].proceed(2)
-    acts[Q].proceed(1, 1)
     acts[V].proceed(2)
 
     def whole(index, h):
@@ -230,7 +226,7 @@
 
     lane = lax.broadcasted_iota(jnp.int32, (rows, rows), 1)
     table = jnp.zeros((rows, rows), F32)
-    mixes, scales, deltas = [], [], []
+    mixes, scales, logs, deltas = [], [], [], []
     for h in range(heads):
         scores = dot_t(act[Q, me, :, lanes(h)], whole(K, h))
         top = jnp.max(scores, axis=-1, keepdims=True)
@@ -238,18 +234,24 @@
         total = jnp.sum(part, axis=-1, keepdims=True)
         expo[h] = part
         mix = (dot(part.astype(BF16), whole(V, h)) / total).astype(BF16)
-        grad = act[O, me, :, lanes(h)]
-        delta = jnp.sum(grad.astype(F32) * mix.astype(F32), axis=-1, keepdims=True)
-        table = jnp.where(lane == h, top + jnp.log(total), table)
-        table = jnp.where(lane == heads + h, delta, table)
         mixes.append(mix)
         scales.append(1.0 / total)
+        logs.append(top + jnp.log(total))
+        if h == 0:
+            weights[O].proceed(1, 1)
+            acts[Q].proceed(1, 1)
+        if h == min(1, heads - 1):
+            weights[O].proceed(2, 2)
+    acts[Q].proceed(2, 2)
+    weights[O].proceed(3)
+    act[O, me] = project(cot, O).astype(BF16)
+    acts[O].begin()
+    for h in range(heads):
+        grad = act[O, me, :, lanes(h)]
+        delta = jnp.sum(grad.astype(F32) * mixes[h].astype(F32), axis=-1, keepdims=True)
+        table = jnp.where(lane == h, logs[h], table)
+        table = jnp.where(lane == heads + h, delta, table)
         deltas.append(delta)
-        if h == 0:
-            acts[O].proceed(1, 1)
-            acts[Q].proceed(2, 2)
-        if h == min(1, heads - 1):
-            acts[O].proceed(2, 2)
     stats[me] = jnp.transpose(table)[: stats.shape[1]]
     sent = []
     for mask in range(1, seq):
@@ -311,7 +313,11 @@
         query_raw_grad.append(
             head_back(query_grad, query_unit[h], query_inverse[h], qg_ref[lanes(h)][None, :], factor)
         )
-    acts[Q].proceed(3)
+        if h == 0:
+            acts[O].proceed(1, 1)
+            acts[Q].proceed(3)
+        if h == min(1, heads - 1):
+            acts[O].proceed(2, 2)
     acts[O].proceed(3)
     for copy in sent:
         copy.wait_recv()
@@ -549,7 +555,7 @@
             kg,
         )
     )
-    steps = 4 if width % 512 == 0 and depth % 32 == 0 else 1
+    steps = 2 if width % 256 == 0 and depth % 16 == 0 else 1
     across = pl.BlockSpec((rows, width // steps), lambda i: (0, i))
     down = pl.BlockSpec((depth // steps, cols), lambda i: (i, 0))
     return tuple(

time: 121 us -> 120 us (level)
    pallas_call x1, Pallas kernels: 4.16 us -> 2.92 us  [body(): pl.pallas_call(finish, grid=(steps,), out_shape=(jax.ShapeDtypeStruct((ro...]
where the time goes in v3:
time: 120 us
  Pallas kernels  119 us (99%)
    pallas_call x1, Pallas kernels, body(): pl.pallas_call(functools.partial(kernel, seq, head), out_shape=(jax.Shape...  116 us
    pallas_call x1, Pallas kernels, body(): pl.pallas_call(finish, grid=(steps,), out_shape=(jax.ShapeDtypeStruct((ro...  2.92 us

profile of v3, /device:TPU:0, one launch (start us, length us, event | category | flops | bytes accessed | tf_op | source)
XLA Modules:
  0.0 119.8 jit_solution(16249732164404732138)
XLA Ops:
  0.6 116.3 %shard_map.122 = (bf16[128,3072]{1,0:T(8,128)(2,1)}, f32[128,128]{1,0:T(8,128)}, f32[384,384]{1,0:T(8,128)}) custom-call(bf16[128,3072]{1,0:T(8,128)(2,1)} %hidden_ref.1, bf16[128,3072]{1,0:T(8,128)(2,1)} %cot_hbm.1, f32[1,3072]{1,0:T(1,128)} %bitcast.3, f32[1,3072]{1,0:T(1,128)} %bitcast.5, f32[1,3072]{1,0:T(1,128)} %bitcast.6, bf16[384,384]{1,0:T(8,128)(2,1)} %qw_ref.1, ...), custom_call_target="tpu_custom_call" | custom-call | tf_op jit(solution)/shard_map/pallas_call | solution.py:503
  116.9 2.9 %shard_map.123 = (bf16[128,3072]{1,0:T(8,128)(2,1)}, f32[384,384]{1,0:T(8,128)}) custom-call(bf16[128,3072]{1,0:T(8,128)(2,1)} %hidden_ref.1, bf16[128,3072]{1,0:T(8,128)(2,1)} %get-tuple-element.5.total_ref, f32[1,3072]{1,0:T(1,128)} %bitcast.4, f32[128,128]{1,0:T(8,128)} %get-tuple-element.6.rowstat_ref, f32[384,384]{1,0:T(8,128)} %get-tuple-element.7.outproj_ref), custom_call_target="tpu_custom_call" | custom-call | tf_op jit(solution)/shard_map/pallas_call | solution.py:562

commit v4 on v3

--- a/solution.py
+++ b/solution.py
@@ -242,6 +242,50 @@
             acts[Q].proceed(1, 1)
         if h == min(1, heads - 1):
             weights[O].proceed(2, 2)
+    mix_flat = jnp.concatenate(mixes, axis=1)
+    half = depth // 2
+    orders = scatter_orders(seq)
+    moves = {}
+    for side in range(2):
+        for mask in range(1, seq):
+            first = [d for d in orders[side] if mask & d][0]
+            moves[side, mask] = pltpu.make_async_remote_copy(
+                src_ref=acc.at[flipped(me, mask), pl.ds(side * half, half)],
+                dst_ref=rbuf.at[mask, pl.ds(side * half, half)],
+                send_sem=rsend.at[side, mask],
+                recv_sem=rrecv.at[side, mask],
+                device_id={"seq": flipped(me, first)},
+                device_id_type=mesh_ids,
+            )
+
+    def stage(level):
+        out = []
+        for side in range(2):
+            done = sum(orders[side][:level])
+            d = orders[side][level]
+            out += [(side, m, d) for m in range(1, seq) if m & d and not m & done]
+        return out
+
+    def scatter_send(level):
+        for side, mask, _ in stage(level):
+            moves[side, mask].start()
+
+    def scatter_add(level):
+        for side, mask, d in stage(level):
+            moves[side, mask].wait_recv()
+            span = pl.ds(side * half, half)
+            slot = flipped(me, mask ^ d)
+            total = acc[slot, span].astype(F32) + rbuf[mask, span].astype(F32)
+            if mask == d and level == len(orders[0]) - 1:
+                outproj_ref[span, :] = total
+            else:
+                acc[slot, span] = total.astype(BF16)
+
+    levels = len(orders[0])
+    for j in range(seq):
+        acc[j] = dot(cot_t[j * depth : (j + 1) * depth, :], mix_flat).astype(BF16)
+    scatter_send(0)
+
     acts[Q].proceed(2, 2)
     weights[O].proceed(3)
     act[O, me] = project(cot, O).astype(BF16)
@@ -266,45 +310,6 @@
         copy.start()
         sent.append(copy)
 
-    mix_flat = jnp.concatenate(mixes, axis=1)
-    half = depth // 2
-    orders = scatter_orders(seq)
-    moves = {}
-    for side in range(2):
-        for mask in range(1, seq):
-            first = [d for d in orders[side] if mask & d][0]
-            moves[side, mask] = pltpu.make_async_remote_copy(
-                src_ref=acc.at[flipped(me, mask), pl.ds(side * half, half)],
-                dst_ref=rbuf.at[mask, pl.ds(side * half, half)],
-                send_sem=rsend.at[side, mask],
-                recv_sem=rrecv.at[side, mask],
-                device_id={"seq": flipped(me, first)},
-                device_id_type=mesh_ids,
-            )
-
-    def stage(level):
-        out = []
-        for side in range(2):
-            done = sum(orders[side][:level])
-            d = orders[side][level]
-            out += [(side, m, d) for m in range(1, seq) if m & d and not m & done]
-        return out
-
-    def scatter_send(level):
-        for side, mask, _ in stage(level):
-            moves[side, mask].start()
-
-    def scatter_add(level):
-        for side, mask, d in stage(level):
-            moves[side, mask].wait_recv()
-            span = pl.ds(side * half, half)
-            slot = flipped(me, mask ^ d)
-            total = acc[slot, span].astype(F32) + rbuf[mask, span].astype(F32)
-            if mask == d and level == len(orders[0]) - 1:
-                outproj_ref[span, :] = total
-            else:
-                acc[slot, span] = total.astype(BF16)
-
     query_raw_grad, key_raw_grad, value_raw_grad = [], [], []
     for h in range(heads):
         prob_grad = dot_t(act[O, me, :, lanes(h)], whole(V, h))
@@ -319,6 +324,9 @@
         if h == min(1, heads - 1):
             acts[O].proceed(2, 2)
     acts[O].proceed(3)
+    if levels > 1:
+        scatter_add(0)
+        scatter_send(1)
     for copy in sent:
         copy.wait_recv()
     for h in range(heads):
@@ -423,33 +431,21 @@
         middle[p] = middle[p] + jnp.sum(scaled, axis=-1, keepdims=True)
         along[p] = along[p] + jnp.sum(scaled * unit, axis=-1, keepdims=True)
 
-    levels = len(orders[0])
-    early = max(chunks // 2, 1)
-    share = -(-seq // early)
     for c in range(chunks + 3):
         if c < chunks:
             own_part(c)
-        for j in range(c * share, min((c + 1) * share, seq)):
-            acc[j] = dot(cot_t[j * depth : (j + 1) * depth, :], mix_flat).astype(BF16)
-        if c == early - 1:
-            scatter_send(0)
         for p in range(parts):
             if 1 <= c <= chunks and mid > 1:
                 pass_in((c - 1) * parts + p)
             if c >= 3:
                 pass_out((c - 3) * parts + p)
-        if c == early + 1:
-            scatter_add(0)
-            if levels > 1:
-                scatter_send(1)
-        if c == chunks and levels > 2:
+        if c == min(2, chunks) and levels > 2:
             scatter_add(1)
             scatter_send(2)
     for level in range(min(levels - 1, 2), levels):
         if level > 2:
             scatter_send(level)
-        if level > 0:
-            scatter_add(level)
+        scatter_add(level)
 
     column = lax.broadcasted_iota(jnp.int32, (rows, 128), 1)
     rowstat = jnp.where(column == 0, mean, inverse)

time: 120 us -> 119 us (level)
  no operation moved by 1% of the time
where the time goes in v4:
time: 119 us
  Pallas kernels  118 us (99%)
    pallas_call x1, Pallas kernels, body(): pl.pallas_call(functools.partial(kernel, seq, head), out_shape=(jax.Shape...  115 us
    pallas_call x1, Pallas kernels, body(): pl.pallas_call(finish, grid=(steps,), out_shape=(jax.ShapeDtypeStruct((ro...  2.92 us

profile of v4, /device:TPU:0, one launch (start us, length us, event | category | flops | bytes accessed | tf_op | source)
XLA Modules:
  0.0 118.8 jit_solution(11080165468722367560)
XLA Ops:
  0.6 115.2 %shard_map.122 = (bf16[128,3072]{1,0:T(8,128)(2,1)}, f32[128,128]{1,0:T(8,128)}, f32[384,384]{1,0:T(8,128)}) custom-call(bf16[128,3072]{1,0:T(8,128)(2,1)} %hidden_ref.1, bf16[128,3072]{1,0:T(8,128)(2,1)} %cot_hbm.1, f32[1,3072]{1,0:T(1,128)} %bitcast.3, f32[1,3072]{1,0:T(1,128)} %bitcast.5, f32[1,3072]{1,0:T(1,128)} %bitcast.6, bf16[384,384]{1,0:T(8,128)(2,1)} %qw_ref.1, ...), custom_call_target="tpu_custom_call" | custom-call | tf_op jit(solution)/shard_map/pallas_call | solution.py:499
  115.9 2.9 %shard_map.123 = (bf16[128,3072]{1,0:T(8,128)(2,1)}, f32[384,384]{1,0:T(8,128)}) custom-call(bf16[128,3072]{1,0:T(8,128)(2,1)} %hidden_ref.1, bf16[128,3072]{1,0:T(8,128)(2,1)} %get-tuple-element.5.total_ref, f32[1,3072]{1,0:T(1,128)} %bitcast.4, f32[128,128]{1,0:T(8,128)} %get-tuple-element.6.rowstat_ref, f32[384,384]{1,0:T(8,128)} %get-tuple-element.7.outproj_ref), custom_call_target="tpu_custom_call" | custom-call | tf_op jit(solution)/shard_map/pallas_call | solution.py:558
